TPU v7x, 32 devices: a whole 2x2x4 slice. The times are simulated.
32 devices in a mesh: head: 4 (over y, core), tok: 8 (over z, x).
Axes of the slice: x: 2, y: 2, z: 4, core: 2. Of those that a mesh axis runs over, the one named last changes fastest.
Arguments:
- hires_tokens: bfloat16 [32768, 1024], P('tok'), may hold values from -6 to 6
- lowres_tokens: bfloat16 [2048, 1024], P('tok'), may hold values from -6 to 6
- norm_gain: float32 [1024], replicated, may hold values from 0.1 to 1.9
- w_cross_q: bfloat16 [1024, 1024], P(None, 'head'), may hold values from -0.1875 to 0.1875
- w_low_kv: bfloat16 [1024, 2, 1024], P(None, None, 'head'), may hold values from -0.1875 to 0.1875
- w_view_qkv: bfloat16 [1024, 3, 1024], P(None, None, 'head'), may hold values from -0.1875 to 0.1875
- w_out: bfloat16 [2, 1024, 1024], P(None, 'head'), may hold values from -0.125 to 0.125
- block_lists: int32 [256, 8], P('tok'), may hold values from 0 to 15, as said below
- block_counts: int32 [256], P('tok'), may hold values from 1 to 8, as said below
Outputs:
- layer_out: bfloat16 [32768, 1024], P('tok', 'head')
Inputs may be any that keep to these rules, and one draw needn't show every extreme that they name: `block_lists`: each row names 8 distinct low-resolution blocks; only the first block_counts entries of a row are used. `block_counts`: in every draw there is at least one index of tok all of whose query blocks use all 8 entries; query blocks of the other indices may use any count from 1 to 8.
All inputs are finite; a program needn't handle non-finite values.
Results may differ from a plain program's by a relative error of at most 0.009.
Values may be sent and summed in bfloat16 or wider, within the bound.
No kernel may reach another device: no remote copies, remote signals or barrier semaphores. Data moves between devices by JAX's collectives and lax.ppermute only.
A program may use at most 128 MiB of HBM per device.

v0:
```python
import functools
import math

import jax
import jax.numpy as jnp
from jax import lax
from jax.experimental import pallas as pl
from jax.experimental.pallas import tpu as pltpu
from jax.sharding import PartitionSpec as P

HD = 128
VIEWS = 8
BLOCK = 128
LOG2_SCALE = math.log2(math.e) / math.sqrt(HD)
VMEM_BYTES = 60 * 1024 * 1024
CONTRACT_LAST = (((1,), (1,)), ((), ()))


def rms_rows(row_block, norm_gain):
    values = row_block.astype(jnp.float32)
    factor = lax.rsqrt(jnp.mean(values * values, axis=-1, keepdims=True) + 1e-06)
    return (values * factor * norm_gain).astype(jnp.bfloat16)


def f32_dot(left, right):
    return jnp.dot(left, right, preferred_element_type=jnp.float32)


def block_diagonal(tiles):
    rows = []
    for index, tile in enumerate(tiles):
        zero = jnp.zeros_like(tile)
        rows.append(
            jnp.concatenate([tile if k == index else zero for k in range(len(tiles))], axis=1)
        )
    return jnp.concatenate(rows, axis=0)


def ring_place(tok, n_tok):
    half = lax.div(tok, 2)
    return jnp.where(lax.rem(tok, 2) == 0, half, n_tok - 1 - half)


def cross_kernel(halves, lists_ref, counts_ref, tok_ref, tokens_ref, gain_ref, wq_ref, *refs):
    kv_refs, out_refs = refs[: -4 - halves], refs[-4 - halves : -4]
    k_ref, vt_ref, q_ref, mixed_ref = refs[-4:]
    step = pl.program_id(0)
    rows, cols = mixed_ref.shape
    heads = cols // HD
    per_step = rows // BLOCK
    listed = lists_ref.shape[1]

    @pl.when(step == 0)
    def _():
        n_tok = len(kv_refs)
        for offset, kv_ref in enumerate(kv_refs):
            chunk = kv_ref.shape[0]
            place = lax.rem(ring_place(tok_ref[0], n_tok) + offset, n_tok)
            home = jnp.where(place < (n_tok + 1) // 2, 2 * place, 2 * (n_tok - 1 - place) + 1)
            start = pl.multiple_of(home * chunk, BLOCK)
            k_ref[pl.ds(start, chunk), :] = kv_ref[:, :cols]
            vt_ref[:, pl.ds(start, chunk)] = kv_ref[:, cols:].T

    normed = rms_rows(tokens_ref[...], gain_ref[...])
    q_ref[...] = (f32_dot(normed, wq_ref[...]) * LOG2_SCALE).astype(jnp.bfloat16)

    def one_block(local, carry):
        block = step * per_step + local
        row_start = pl.multiple_of(local * BLOCK, BLOCK)
        count = counts_ref[block]
        first = lists_ref[block, 0]
        starts = [
            pl.multiple_of(jnp.where(j < count, lists_ref[block, j], first) * BLOCK, BLOCK)
            for j in range(listed)
        ]
        query = block_diagonal(
            [q_ref[pl.ds(row_start, BLOCK), h * HD : (h + 1) * HD] for h in range(heads)]
        )
        keys = jnp.concatenate([k_ref[pl.ds(s, BLOCK), :] for s in starts], axis=0)
        scores = lax.dot_general(keys, query, CONTRACT_LAST, preferred_element_type=jnp.float32)
        top = jnp.max(scores, axis=0, keepdims=True)
        weights = []
        total = jnp.zeros_like(top)
        for j in range(listed):
            shift = top + jnp.where(j < count, 0.0, 1e30)
            weight = jnp.exp2(scores[j * BLOCK : (j + 1) * BLOCK] - shift)
            total = total + jnp.sum(weight, axis=0, keepdims=True)
            weights.append(weight.astype(jnp.bfloat16))
        values_t = jnp.concatenate([vt_ref[:, pl.ds(s, BLOCK)] for s in starts], axis=1)
        mixed_t = f32_dot(values_t, jnp.concatenate(weights, axis=0)) / total
        for h in range(heads):
            part = slice(h * HD, (h + 1) * HD)
            mixed_ref[pl.ds(row_start, BLOCK), part] = mixed_t[part, part].T.astype(jnp.bfloat16)
        return carry

    lax.fori_loop(0, per_step, one_block, 0, unroll=True)
    half_steps = pl.num_programs(0) // halves
    for half, out_ref in enumerate(out_refs):
        @pl.when(lax.div(step, half_steps) == half)
        def _():
            out_ref[...] = mixed_ref[...]


def cross_attention(hires_tokens, gain, w_cross_q, kv_chunks, block_lists, block_counts):
    tok_index = lax.axis_index("tok").reshape(1)
    tok_rows, width = hires_tokens.shape
    cols = w_cross_q.shape[1]
    chunk = kv_chunks[0].shape[0]
    low_rows = chunk * len(kv_chunks)
    halves = 1
    rows = math.gcd(tok_rows // halves, 4 * BLOCK)
    half_steps = tok_rows // halves // rows
    return pl.pallas_call(
        functools.partial(cross_kernel, halves),
        out_shape=[jax.ShapeDtypeStruct((tok_rows // halves, cols), jnp.bfloat16)] * halves,
        grid_spec=pltpu.PrefetchScalarGridSpec(
            num_scalar_prefetch=3,
            grid=(tok_rows // rows,),
            in_specs=[
                pl.BlockSpec((rows, width), lambda i, *_: (i, 0)),
                pl.BlockSpec((1, width), lambda i, *_: (0, 0)),
                pl.BlockSpec((width, cols), lambda i, *_: (0, 0)),
            ]
            + [pl.BlockSpec((chunk, 2 * cols), lambda i, *_: (0, 0)) for _ in kv_chunks],
            out_specs=[
                pl.BlockSpec(
                    (rows, cols),
                    lambda i, *_, half=half: (jnp.clip(i - half * half_steps, 0, half_steps - 1), 0),
                )
                for half in range(halves)
            ],
            scratch_shapes=[
                pltpu.VMEM((low_rows, cols), jnp.bfloat16),
                pltpu.VMEM((cols, low_rows), jnp.bfloat16),
                pltpu.VMEM((rows, cols), jnp.bfloat16),
                pltpu.VMEM((rows, cols), jnp.bfloat16),
            ],
        ),
        compiler_params=pltpu.CompilerParams(vmem_limit_bytes=VMEM_BYTES),
        cost_estimate=pl.CostEstimate(
            flops=2 * tok_rows * cols * (width + 2 * block_lists.shape[1] * BLOCK * 2),
            bytes_accessed=2 * tok_rows * (width + cols),
            transcendentals=tok_rows * block_lists.shape[1] * BLOCK * (cols // HD),
        ),
        name="cross",
    )(block_lists, block_counts, tok_index, hires_tokens, gain, w_cross_q, *kv_chunks)


def view_kernel(tokens_ref, gain_ref, w_ref, wo_ref, out_ref, normed_ref, qkv_ref, mixed_ref):
    parts, sources, run, cols = out_ref.shape
    part_index = pl.program_id(0)
    heads = cols // HD
    rows = sources * run
    pixels = rows // VIEWS
    group = math.gcd(pixels, 32)
    tile = math.gcd(rows, 512)

    @pl.when(pl.program_id(0) == 0)
    def _():
        gain = gain_ref[...]
        step = math.gcd(sources, max(1, tile // run))
        for s in range(0, sources, step):
            tokens = tokens_ref[s : s + step].reshape(step * run, gain.shape[1])
            normed_ref[s * run : (s + step) * run] = rms_rows(tokens, gain)

    for start in range(0, rows, tile):
        stop = start + tile
        tokens = normed_ref[start:stop]
        for k in range(3):
            projected = f32_dot(tokens, w_ref[0, k])
            if k == 0:
                projected = projected * LOG2_SCALE
            qkv_ref[start:stop, k * cols : (k + 1) * cols] = projected.astype(jnp.bfloat16)
    size = VIEWS * group
    row_pixel = lax.broadcasted_iota(jnp.int32, (size, size), 0) % group
    col_pixel = lax.broadcasted_iota(jnp.int32, (size, size), 1) % group
    same = row_pixel == col_pixel

    def gathered(first, column):
        part = slice(column, column + HD)
        return jnp.concatenate(
            [qkv_ref[v * pixels + first : v * pixels + first + group, part] for v in range(VIEWS)],
            axis=0,
        )

    for first in range(0, pixels, group):
        for h in range(heads):
            query = gathered(first, h * HD)
            key = gathered(first, cols + h * HD)
            value = gathered(first, 2 * cols + h * HD)
            scores = lax.dot_general(query, key, CONTRACT_LAST, preferred_element_type=jnp.float32)
            scores = jnp.where(same, scores, -1e30)
            weight = jnp.exp2(scores - jnp.max(scores, axis=1, keepdims=True))
            value_and_one = jnp.concatenate([value, jnp.ones_like(value)], axis=1)
            mixed_and_total = f32_dot(weight.astype(jnp.bfloat16), value_and_one)
            mixed = (mixed_and_total[:, :HD] / mixed_and_total[:, HD:]).astype(jnp.bfloat16)
            for v in range(VIEWS):
                rows_of = slice(v * pixels + first, v * pixels + first + group)
                mixed_ref[part_index, rows_of, h * HD : (h + 1) * HD] = (
                    mixed[v * group : (v + 1) * group]
                )

    @pl.when(part_index == parts - 1)
    def _():
        step = math.gcd(sources, max(1, tile // run))
        for s in range(0, sources, step):
            rows_of = slice(s * run, (s + step) * run)
            for column in range(parts):
                w_rows = slice(column * cols, (column + 1) * cols)
                term = f32_dot(mixed_ref[0, rows_of], wo_ref[0, 0, w_rows])
                for g in range(1, parts):
                    term = term + f32_dot(mixed_ref[g, rows_of], wo_ref[g, 0, w_rows])
                out_ref[column, s : s + step] = term.astype(jnp.bfloat16).reshape(step, run, cols)


def view_attention(tokens, gain, weights):
    n_tok, run, width = tokens.shape
    parts, _, _, cols = weights.shape
    rows = n_tok * run
    return pl.pallas_call(
        view_kernel,
        out_shape=jax.ShapeDtypeStruct((parts, n_tok, run, cols), jnp.bfloat16),
        grid=(parts,),
        in_specs=[
            pl.BlockSpec((n_tok, run, width), lambda i: (0, 0, 0)),
            pl.BlockSpec((1, width), lambda i: (0, 0)),
            pl.BlockSpec((1, 3, width, cols), lambda i: (i, 0, 0, 0)),
            pl.BlockSpec((parts, 1, width, cols), lambda i: (0, 4, 0, 0)),
        ],
        out_specs=pl.BlockSpec((parts, n_tok, run, cols), lambda i: (0, 0, 0, 0)),
        scratch_shapes=[
            pltpu.VMEM((rows, width), jnp.bfloat16),
            pltpu.VMEM((rows, 3 * cols), jnp.bfloat16),
            pltpu.VMEM((parts, rows, cols), jnp.bfloat16),
        ],
        compiler_params=pltpu.CompilerParams(vmem_limit_bytes=VMEM_BYTES),
        cost_estimate=pl.CostEstimate(
            flops=2 * rows * (parts * cols * (3 * width + 512) + width * width),
            bytes_accessed=2 * (2 * rows * width + 4 * parts * width * cols),
            transcendentals=parts * rows * 512,
        ),
        name="view",
    )(tokens, gain, weights, weights)


def final_kernel(index_ref, tokens_ref, cross_ref, view_ref, w_ref, out_ref):
    total = tokens_ref[...].astype(jnp.float32) + view_ref[...].astype(jnp.float32)
    for g in range(cross_ref.shape[0]):
        total = total + f32_dot(cross_ref[g], w_ref[g, 0])
    out_ref[...] = total.astype(jnp.bfloat16)


def final_sum(head_index, hires_tokens, cross_all, view_term, weights):
    parts, tok_rows, cols = cross_all.shape
    rows = math.gcd(tok_rows, 512)
    own = pl.BlockSpec((rows, cols), lambda i, index: (i, 0))
    return pl.pallas_call(
        final_kernel,
        out_shape=jax.ShapeDtypeStruct((tok_rows, cols), jnp.bfloat16),
        grid_spec=pltpu.PrefetchScalarGridSpec(
            num_scalar_prefetch=1,
            grid=(tok_rows // rows,),
            in_specs=[
                pl.BlockSpec((rows, cols), lambda i, index: (i, index[0])),
                pl.BlockSpec((parts, rows, cols), lambda i, index: (0, i, 0)),
                own,
                pl.BlockSpec((parts, 1, cols, cols), lambda i, index: (0, 3, index[0], 0)),
            ],
            out_specs=own,
        ),
        compiler_params=pltpu.CompilerParams(vmem_limit_bytes=VMEM_BYTES),
        cost_estimate=pl.CostEstimate(
            flops=2 * parts * tok_rows * cols * cols,
            bytes_accessed=2 * tok_rows * cols * (parts + 3),
            transcendentals=0,
        ),
        name="final",
    )(head_index.reshape(1), hires_tokens, cross_all, view_term, weights)


def ring_chunks(own, n_tok):
    order = list(range(0, n_tok, 2)) + list(range(1, n_tok, 2))[::-1]
    upward = [(order[p], order[(p + 1) % n_tok]) for p in range(n_tok)]
    downward = [(order[p], order[p - 1]) for p in range(n_tok)]
    behind, ahead = [own], [own]
    for step in range(n_tok // 2):
        behind.append(lax.ppermute(behind[-1], "tok", upward))
        if step < (n_tok - 1) // 2:
            ahead.append(lax.ppermute(ahead[-1], "tok", downward))
    return ahead + behind[:0:-1]


def shards(
    n_head,
    n_tok,
    hires_tokens,
    lowres_tokens,
    norm_gain,
    w_cross_q,
    w_low_kv,
    w_view_qkv,
    w_out,
    block_lists,
    block_counts,
):
    tok_rows, width = hires_tokens.shape
    cols = w_cross_q.shape[1]
    quarter = tok_rows // n_head
    head_index = lax.axis_index("head")
    gain = norm_gain.reshape(1, width)

    run = quarter // n_tok

    own_weights = jnp.concatenate(
        [
            w_view_qkv.transpose(1, 0, 2),
            w_out.reshape(2, cols, n_head, cols).transpose(0, 2, 1, 3).reshape(2, width, cols),
        ],
        axis=0,
    )
    weights = lax.all_gather(own_weights, "head", axis=0, tiled=False)
    low_kv = f32_dot(
        rms_rows(lowres_tokens, norm_gain), w_low_kv.reshape(width, 2 * cols)
    ).astype(jnp.bfloat16)
    kv_chunks = ring_chunks(low_kv, n_tok)
    sent = lax.dynamic_slice_in_dim(hires_tokens, head_index * quarter, quarter, 0)
    kv_chunks, sent = lax.optimization_barrier((kv_chunks, sent))

    arrived = lax.all_to_all(
        sent.reshape(n_tok, run, width), "tok", split_axis=0, concat_axis=0, tiled=True
    )
    (cross_out,) = cross_attention(
        hires_tokens, gain, w_cross_q, kv_chunks, block_lists, block_counts
    )
    cross_out, arrived = lax.optimization_barrier((cross_out, arrived))
    cross_all = lax.all_gather(cross_out, "head", axis=0, tiled=False)
    view_term = lax.all_to_all(
        view_attention(arrived, gain, weights).reshape(n_head * n_tok, run, cols),
        ("head", "tok"), split_axis=0, concat_axis=0, tiled=True,
    )
    return final_sum(
        head_index, hires_tokens, cross_all, view_term.reshape(tok_rows, cols), weights
    )


def solution(mesh):
    in_specs = (
        P("tok", None),
        P("tok", None),
        P(),
        P(None, "head"),
        P(None, None, "head"),
        P(None, None, "head"),
        P(None, "head", None),
        P("tok", None),
        P("tok"),
    )
    out_specs = P("tok", "head")
    body = functools.partial(shards, mesh.shape["head"], mesh.shape["tok"])
    return jax.shard_map(body, mesh=mesh, in_specs=in_specs, out_specs=out_specs, check_vma=False)
```

profile of v0, /device:TPU:0, one launch (start us, length us, event | category | flops | bytes accessed | tf_op | source)
XLA Modules:
  0.0 190.7 jit_solution(13696438004885627740)
XLA Ops:
  6.5 0.0 all-gather.7.cloned.1.call-start
  6.5 1.4 copy.17
  8.0 0.3 copy-done.2
  8.3 1.7 pad_maximum_fusion
  10.0 0.0 all-gather.7.cloned.1.call-update
  10.0 1.2 copy-done.3
  11.2 0.2 copy.15
  11.5 0.0 copy-done.4
  11.5 0.2 fusion
  11.7 0.0 copy-done.14
  11.7 0.5 convolution_convert_fusion.refs_0_
  12.2 0.0 copy-start.6
  12.2 3.1 %collective-permute-start.3 = (bf16[256,512]{1,0:T(8,128)(2,1)S(1)}, bf16[256,512]{1,0:T(8,128)(2,1)S(1)}, u32[]{:S(2)}, u32[]{:S(2)}) collective-permute-start(bf16[256,512]{1,0:T(8,128)(2,1)S(1)} %convolution_convert_fusion.refs_0_), channel_id=1, source_target_pairs={{0,2},{2,4},{4,6},{6,7},{7,5},{5,3},{3,1},{1,0},{8,10},{10,12},{12... | collective-permute-start | bytes 786440 | tf_op jit(solution)/shard_map/ppermute | solution.py:287
  15.2 0.0 collective-permute-start
  15.2 6.2 %collective-permute-done.3.refs_7_ = bf16[256,512]{1,0:T(8,128)(2,1)S(1)} collective-permute-done((bf16[256,512]{1,0:T(8,128)(2,1)S(1)}, bf16[256,512]{1,0:T(8,128)(2,1)S(1)}, u32[]{:S(2)}, u32[]{:S(2)}) %collective-permute-start.3) | collective-permute-done | bytes 262176 | tf_op jit(solution)/shard_map/ppermute | solution.py:287
  21.5 1.8 collective-permute-start.4
  23.3 0.0 collective-permute-done.refs_1_
  23.3 0.2 collective-permute-start.1
  23.5 5.5 %collective-permute-done.4.refs_6_ = bf16[256,512]{1,0:T(8,128)(2,1)S(1)} collective-permute-done((bf16[256,512]{1,0:T(8,128)(2,1)S(1)}, bf16[256,512]{1,0:T(8,128)(2,1)S(1)}, u32[]{:S(2)}, u32[]{:S(2)}) %collective-permute-start.4) | collective-permute-done | bytes 262176 | tf_op jit(solution)/shard_map/ppermute | solution.py:287
  29.0 1.5 collective-permute-start.5
  30.5 0.0 collective-permute-done.1.refs_2_
  30.5 0.5 collective-permute-start.2
  31.0 4.6 %collective-permute-done.5.refs_5_ = bf16[256,512]{1,0:T(8,128)(2,1)S(1)} collective-permute-done((bf16[256,512]{1,0:T(8,128)(2,1)S(1)}, bf16[256,512]{1,0:T(8,128)(2,1)S(1)}, u32[]{:S(2)}, u32[]{:S(2)}) %collective-permute-start.5) | collective-permute-done | bytes 262176 | tf_op jit(solution)/shard_map/ppermute | solution.py:287
  35.6 1.2 collective-permute-start.6
  36.8 3.1 %constant_dynamic-slice_fusion = bf16[1024,1024]{1,0:T(8,128)(2,1)} fusion(bf16[4096,1024]{1,0:T(8,128)(2,1)} %tokens_ref.3, s32[]{:T(128)S(6)} %select_n.3), kind=kLoop, calls=%fused_computation.11 | loop fusion | bytes 4194308 | tf_op jit(solution)/shard_map/dynamic_slice | solution.py:326
  40.0 0.0 copy-done.6
  40.0 0.0 copy-done.7
  40.0 0.0 copy-done.8
  40.0 0.0 copy-done.9
  40.0 0.0 collective-permute-done.2.refs_3_
  40.0 0.0 copy-start.12
  40.0 2.0 %collective-permute-done.6.refs_4_ = bf16[256,512]{1,0:T(8,128)(2,1)S(1)} collective-permute-done((bf16[256,512]{1,0:T(8,128)(2,1)S(1)}, bf16[256,512]{1,0:T(8,128)(2,1)S(1)}, u32[]{:S(2)}, u32[]{:S(2)}) %collective-permute-start.6) | collective-permute-done | bytes 262176 | tf_op jit(solution)/shard_map/ppermute | solution.py:287
  42.0 0.0 copy-done.12
  42.0 0.7 copy-done.13
  42.7 5.4 %all-to-all-start = ((bf16[8,128,1024]{2,1,0:T(8,128)(2,1)}), bf16[8,128,1024]{2,1,0:T(8,128)(2,1)S(1)}, u32[]{:S(2)}, u32[]{:S(2)}) async-start(bf16[8,128,1024]{2,1,0:T(8,128)(2,1)} %bitcast.3), calls=%async_computation | async-start | bytes 4194304 | tf_op jit(solution)/shard_map/all_to_all | solution.py:329
  48.2 0.0 all-gather.5.cloned.1.call-start
  48.2 0.7 copy.12.lists_ref
  48.9 26.7 %cross.1 = bf16[4096,256]{1,0:T(8,128)(2,1)} custom-call(s32[32,8]{1,0:T(8,128)} %copy.12.lists_ref, s32[32]{0:T(128)} %counts_ref.1, s32[1]{0:T(128)} %bitcast.1.tok_ref, bf16[4096,1024]{1,0:T(8,128)(2,1)} %tokens_ref.3, f32[1,1024]{1,0:T(1,128)} %bitcast.30, bf16[1024,256]{1,0:T(8,128)(2,1)} %wq_ref.1, bf16[256,512]{1,0:T(8,128)(2,1)} %copy-done.6, ...), custom_call_target="tpu_custom_call" | custom-call | flops 10737418240 | bytes 10485760 | tf_op jit(solution)/shard_map/cross/pallas_call | solution.py:113
  75.6 17.8 %all-to-all-done.tokens_ref = bf16[8,128,1024]{2,1,0:T(8,128)(2,1)S(1)} async-done(((bf16[8,128,1024]{2,1,0:T(8,128)(2,1)}), bf16[8,128,1024]{2,1,0:T(8,128)(2,1)S(1)}, u32[]{:S(2)}, u32[]{:S(2)}) %all-to-all-start) | async-done | bytes 2097184 | tf_op jit(solution)/shard_map/all_to_all | solution.py:329
  93.4 0.0 all-gather.5.cloned.1.call-update
  93.5 0.0 all-gather.7.cloned.1.call-done
  93.5 1.3 copy-done.1
  94.8 17.9 %view.1 = bf16[4,8,128,256]{3,2,1,0:T(8,128)(2,1)} custom-call(bf16[8,128,1024]{2,1,0:T(8,128)(2,1)} %copy-done.1, f32[1,1024]{1,0:T(1,128)} %bitcast.31, bf16[4,5,1024,256]{3,2,1,0:T(8,128)(2,1)} %bitcast.19, bf16[4,5,1024,256]{3,2,1,0:T(8,128)(2,1)} %bitcast.20), custom_call_target="tpu_custom_call" | custom-call | flops 9663676416 | bytes 12582912 | tf_op jit(solution)/shard_map/view/pallas_call | solution.py:220
  112.7 3.5 %all-to-all-start.1 = ((bf16[32,128,256]{2,1,0:T(8,128)(2,1)}), bf16[32,128,256]{2,1,0:T(8,128)(2,1)S(1)}, u32[]{:S(2)}, u32[]{:S(2)}) async-start(bf16[32,128,256]{2,1,0:T(8,128)(2,1)} %bitcast.25), calls=%async_computation.1 | async-start | bytes 4194304 | tf_op jit(solution)/shard_map/all_to_all | solution.py:337
  116.1 57.1 %all-gather.5.cloned.1.call-done = bf16[16384,256]{1,0:T(8,128)(2,1)} async-done(((bf16[4096,256]{1,0:T(8,128)(2,1)}), bf16[16384,256]{1,0:T(8,128)(2,1)}) %all-gather.5.cloned.1.call-update) | async-done | bytes 8388624 | tf_op jit(solution)/shard_map/all_gather | solution.py:336
  173.2 0.0 all-to-all-done.1
  173.3 1.3 copy-done
  174.6 9.3 %final.1 = bf16[4096,256]{1,0:T(8,128)(2,1)} custom-call(s32[1]{0:T(128)} %bitcast.index_ref, bf16[4096,1024]{1,0:T(8,128)(2,1)} %tokens_ref.3, bf16[4,4096,256]{2,1,0:T(8,128)(2,1)} %bitcast.23, bf16[4096,256]{1,0:T(8,128)(2,1)} %bitcast.22, bf16[4,5,1024,256]{3,2,1,0:T(8,128)(2,1)} %bitcast.21), custom_call_target="tpu_custom_call" | custom-call | flops 2147483648 | bytes 14680064 | tf_op jit(solution)/shard_map/final/pallas_call | solution.py:257
  (17 shorter events, 0.0 us)
Async XLA Ops:
  6.5 1.7 copy-start.2
  6.5 87.0 %all-gather.7.cloned.1.call-start = ((), (), s32[]{:S(2)}) async-start(), calls=%async_computation.3 | async-start | bytes 13107200 | tf_op jit(solution)/shard_map/all_gather | solution.py:321
  10.0 1.2 copy-start.3
  10.0 1.5 copy-start.4
  10.0 1.7 copy-start.14
  12.2 27.8 %copy-start.6 = (bf16[256,512]{1,0:T(8,128)(2,1)}, bf16[256,512]{1,0:T(8,128)(2,1)S(1)}, u32[]{:S(2)}) copy-start(bf16[256,512]{1,0:T(8,128)(2,1)S(1)} %convolution_convert_fusion.refs_0_) | copy-start | bytes 786436
  12.2 9.3 %collective-permute-start.3 = (bf16[256,512]{1,0:T(8,128)(2,1)S(1)}, bf16[256,512]{1,0:T(8,128)(2,1)S(1)}, u32[]{:S(2)}, u32[]{:S(2)}) collective-permute-start(bf16[256,512]{1,0:T(8,128)(2,1)S(1)} %convolution_convert_fusion.refs_0_), channel_id=1, source_target_pairs={{0,2},{2,4},{4,6},{6,7},{7,5},{5,3},{3,1},{1,0},{8,10},{10,12},{12... | collective-permute-start | bytes 786440 | tf_op jit(solution)/shard_map/ppermute | solution.py:287
  15.2 8.1 %collective-permute-start = (bf16[256,512]{1,0:T(8,128)(2,1)S(1)}, bf16[256,512]{1,0:T(8,128)(2,1)S(1)}, u32[]{:S(2)}, u32[]{:S(2)}) collective-permute-start(bf16[256,512]{1,0:T(8,128)(2,1)S(1)} %convolution_convert_fusion.refs_0_), channel_id=1, source_target_pairs={{0,1},{2,0},{4,2},{6,4},{7,6},{5,7},{3,5},{1,3},{8,9},{10,8},{12,1... | collective-permute-start | bytes 786440 | tf_op jit(solution)/shard_map/ppermute | solution.py:289
  21.5 18.5 %copy-start.7 = (bf16[256,512]{1,0:T(8,128)(2,1)}, bf16[256,512]{1,0:T(8,128)(2,1)S(1)}, u32[]{:S(2)}) copy-start(bf16[256,512]{1,0:T(8,128)(2,1)S(1)} %collective-permute-done.3.refs_7_) | copy-start | bytes 786436
  21.5 7.5 %collective-permute-start.4 = (bf16[256,512]{1,0:T(8,128)(2,1)S(1)}, bf16[256,512]{1,0:T(8,128)(2,1)S(1)}, u32[]{:S(2)}, u32[]{:S(2)}) collective-permute-start(bf16[256,512]{1,0:T(8,128)(2,1)S(1)} %collective-permute-done.3.refs_7_), channel_id=1, source_target_pairs={{0,2},{2,4},{4,6},{6,7},{7,5},{5,3},{3,1},{1,0},{8,10},{10,12},{12... | collective-permute-start | bytes 786440 | tf_op jit(solution)/shard_map/ppermute | solution.py:287
  23.3 16.7 %copy-start.8 = (bf16[256,512]{1,0:T(8,128)(2,1)}, bf16[256,512]{1,0:T(8,128)(2,1)S(1)}, u32[]{:S(2)}) copy-start(bf16[256,512]{1,0:T(8,128)(2,1)S(1)} %collective-permute-done.refs_1_) | copy-start | bytes 786436
  23.3 7.2 %collective-permute-start.1 = (bf16[256,512]{1,0:T(8,128)(2,1)S(1)}, bf16[256,512]{1,0:T(8,128)(2,1)S(1)}, u32[]{:S(2)}, u32[]{:S(2)}) collective-permute-start(bf16[256,512]{1,0:T(8,128)(2,1)S(1)} %collective-permute-done.refs_1_), channel_id=1, source_target_pairs={{0,1},{2,0},{4,2},{6,4},{7,6},{5,7},{3,5},{1,3},{8,9},{10,8},{12,1... | collective-permute-start | bytes 786440 | tf_op jit(solution)/shard_map/ppermute | solution.py:289
  29.0 11.0 %copy-start.9 = (bf16[256,512]{1,0:T(8,128)(2,1)}, bf16[256,512]{1,0:T(8,128)(2,1)S(1)}, u32[]{:S(2)}) copy-start(bf16[256,512]{1,0:T(8,128)(2,1)S(1)} %collective-permute-done.4.refs_6_) | copy-start | bytes 786436
  29.0 6.7 %collective-permute-start.5 = (bf16[256,512]{1,0:T(8,128)(2,1)S(1)}, bf16[256,512]{1,0:T(8,128)(2,1)S(1)}, u32[]{:S(2)}, u32[]{:S(2)}) collective-permute-start(bf16[256,512]{1,0:T(8,128)(2,1)S(1)} %collective-permute-done.4.refs_6_), channel_id=1, source_target_pairs={{0,2},{2,4},{4,6},{6,7},{7,5},{5,3},{3,1},{1,0},{8,10},{10,12},{12... | collective-permute-start | bytes 786440 | tf_op jit(solution)/shard_map/ppermute | solution.py:287
  30.5 9.5 %copy-start.10 = (bf16[256,512]{1,0:T(8,128)(2,1)}, bf16[256,512]{1,0:T(8,128)(2,1)S(1)}, u32[]{:S(2)}) copy-start(bf16[256,512]{1,0:T(8,128)(2,1)S(1)} %collective-permute-done.1.refs_2_) | copy-start | bytes 786436
  30.5 9.5 %collective-permute-start.2 = (bf16[256,512]{1,0:T(8,128)(2,1)S(1)}, bf16[256,512]{1,0:T(8,128)(2,1)S(1)}, u32[]{:S(2)}, u32[]{:S(2)}) collective-permute-start(bf16[256,512]{1,0:T(8,128)(2,1)S(1)} %collective-permute-done.1.refs_2_), channel_id=1, source_target_pairs={{0,1},{2,0},{4,2},{6,4},{7,6},{5,7},{3,5},{1,3},{8,9},{10,8},{12,1... | collective-permute-start | bytes 786440 | tf_op jit(solution)/shard_map/ppermute | solution.py:289
  35.6 4.4 %copy-start.11 = (bf16[256,512]{1,0:T(8,128)(2,1)}, bf16[256,512]{1,0:T(8,128)(2,1)S(1)}, u32[]{:S(2)}) copy-start(bf16[256,512]{1,0:T(8,128)(2,1)S(1)} %collective-permute-done.5.refs_5_) | copy-start | bytes 786436
  35.6 6.4 %collective-permute-start.6 = (bf16[256,512]{1,0:T(8,128)(2,1)S(1)}, bf16[256,512]{1,0:T(8,128)(2,1)S(1)}, u32[]{:S(2)}, u32[]{:S(2)}) collective-permute-start(bf16[256,512]{1,0:T(8,128)(2,1)S(1)} %collective-permute-done.5.refs_5_), channel_id=1, source_target_pairs={{0,2},{2,4},{4,6},{6,7},{7,5},{5,3},{3,1},{1,0},{8,10},{10,12},{12... | collective-permute-start | bytes 786440 | tf_op jit(solution)/shard_map/ppermute | solution.py:287
  40.0 2.0 %copy-start.12 = (bf16[256,512]{1,0:T(8,128)(2,1)}, bf16[256,512]{1,0:T(8,128)(2,1)S(1)}, u32[]{:S(2)}) copy-start(bf16[256,512]{1,0:T(8,128)(2,1)S(1)} %collective-permute-done.2.refs_3_) | copy-start | bytes 786436
  42.0 0.7 copy-start.13
  42.0 6.2 %copy-start.5 = (s32[32,8]{0,1:T(8,128)S(1)}, s32[32,8]{0,1:T(8,128)}, u32[]{:S(2)}) copy-start(s32[32,8]{0,1:T(8,128)} %param.16) | copy-start | bytes 3076
  42.7 50.7 %all-to-all-start = ((bf16[8,128,1024]{2,1,0:T(8,128)(2,1)}), bf16[8,128,1024]{2,1,0:T(8,128)(2,1)S(1)}, u32[]{:S(2)}, u32[]{:S(2)}) async-start(bf16[8,128,1024]{2,1,0:T(8,128)(2,1)} %bitcast.3), calls=%async_computation | async-start | bytes 4194304 | tf_op jit(solution)/shard_map/all_to_all | solution.py:329
  48.2 125.1 %all-gather.5.cloned.1.call-start = ((), (), s32[]{:S(2)}) async-start(), calls=%async_computation.2 | async-start | bytes 10485760 | tf_op jit(solution)/shard_map/all_gather | solution.py:336
  93.4 1.4 copy-start.1
  112.7 60.6 %all-to-all-start.1 = ((bf16[32,128,256]{2,1,0:T(8,128)(2,1)}), bf16[32,128,256]{2,1,0:T(8,128)(2,1)S(1)}, u32[]{:S(2)}, u32[]{:S(2)}) async-start(bf16[32,128,256]{2,1,0:T(8,128)(2,1)} %bitcast.25), calls=%async_computation.1 | async-start | bytes 4194304 | tf_op jit(solution)/shard_map/all_to_all | solution.py:337
  173.2 1.3 copy-start
Sparse Core Ops, SparseCore 0:
  10.2 72.8 all-gather.6
  93.6 79.6 all-gather.4
where the time goes:
time: 191 us
  waiting for transfers between devices  93.3 us (49%)
  Pallas kernels  53.9 us (28%)
  starting transfers between devices  17.3 us (9%)
  between operations  13.5 us (7%)
  local copies, waits for them, and re-layouts  10.3 us (5%)
  other arithmetic  1.94 us (1%)
    all_gather x1, waiting for transfers between devices, shards(): cross_all = lax.all_gather(cross_out, 'head', axis=0, tiled=False)  57.1 us
    pallas_call x1, Pallas kernels, cross_attention(): pl.pallas_call(functools.partial(cross_kernel, halves), out_shape=[jax.Sh...  26.7 us
    ppermute x4, waiting for transfers between devices, ring_chunks(): behind.append(lax.ppermute(behind[-1], 'tok', upward))  18.3 us
    pallas_call x1, Pallas kernels, view_attention(): pl.pallas_call(view_kernel, out_shape=jax.ShapeDtypeStruct((parts, n_tok,...  17.9 us
    all_to_all x1, waiting for transfers between devices, shards(): lax.all_to_all(sent.reshape(n_tok, run, width), 'tok', split_axis=0, conc...  17.8 us
    pallas_call x1, Pallas kernels, final_sum(): pl.pallas_call(final_kernel, out_shape=jax.ShapeDtypeStruct((tok_rows, co...  9.31 us
    ppermute x4, starting transfers between devices, ring_chunks(): behind.append(lax.ppermute(behind[-1], 'tok', upward))  7.62 us
    unnamed x32, local copies, waits for them, and re-layouts  5.76 us
  transfers between devices with their start and end apart: 11, of which 6 were waited for; matrix products, arithmetic and copies ran while one was open for 2% of the time, Pallas kernels for 23%

commit v1 on v0

--- a/solution.py
+++ b/solution.py
@@ -311,6 +311,10 @@
 
     run = quarter // n_tok
 
+    low_kv = f32_dot(
+        rms_rows(lowres_tokens, norm_gain), w_low_kv.reshape(width, 2 * cols)
+    ).astype(jnp.bfloat16)
+    low_kv, w_view_qkv, w_out = lax.optimization_barrier((low_kv, w_view_qkv, w_out))
     own_weights = jnp.concatenate(
         [
             w_view_qkv.transpose(1, 0, 2),
@@ -319,9 +323,6 @@
         axis=0,
     )
     weights = lax.all_gather(own_weights, "head", axis=0, tiled=False)
-    low_kv = f32_dot(
-        rms_rows(lowres_tokens, norm_gain), w_low_kv.reshape(width, 2 * cols)
-    ).astype(jnp.bfloat16)
     kv_chunks = ring_chunks(low_kv, n_tok)
     sent = lax.dynamic_slice_in_dim(hires_tokens, head_index * quarter, quarter, 0)
     kv_chunks, sent = lax.optimization_barrier((kv_chunks, sent))

time: 191 us -> 191 us (level)
  no operation moved by 1% of the time
where the time goes in v1:
time: 191 us; the launch traced here: 190 us
  waiting for transfers between devices  93.1 us (49%)
  Pallas kernels  53.9 us (28%)
  starting transfers between devices  17.6 us (9%)
  between operations  13.5 us (7%)
  local copies, waits for them, and re-layouts  9.6 us (5%)
  other arithmetic  1.94 us (1%)
    all_gather x1, waiting for transfers between devices, shards(): cross_all = lax.all_gather(cross_out, 'head', axis=0, tiled=False)  57.1 us
    pallas_call x1, Pallas kernels, cross_attention(): pl.pallas_call(functools.partial(cross_kernel, halves), out_shape=[jax.Sh...  26.7 us
    ppermute x4, waiting for transfers between devices, ring_chunks(): behind.append(lax.ppermute(behind[-1], 'tok', upward))  18.1 us
    pallas_call x1, Pallas kernels, view_attention(): pl.pallas_call(view_kernel, out_shape=jax.ShapeDtypeStruct((parts, n_tok,...  17.9 us
    all_to_all x1, waiting for transfers between devices, shards(): lax.all_to_all(sent.reshape(n_tok, run, width), 'tok', split_axis=0, conc...  17.8 us
    pallas_call x1, Pallas kernels, final_sum(): pl.pallas_call(final_kernel, out_shape=jax.ShapeDtypeStruct((tok_rows, co...  9.31 us
    ppermute x4, starting transfers between devices, ring_chunks(): behind.append(lax.ppermute(behind[-1], 'tok', upward))  7.76 us
    unnamed x32, local copies, waits for them, and re-layouts  6.42 us
  transfers between devices with their start and end apart: 11, of which 6 were waited for; matrix products, arithmetic and copies ran while one was open for 2% of the time, Pallas kernels for 23%

profile of v1, /device:TPU:0, one launch (start us, length us, event | category | flops | bytes accessed | tf_op | source)
XLA Modules:
  0.0 190.1 jit_solution(1135058106457622404)
XLA Ops:
  6.5 0.0 all-gather.7.cloned.1.call-start
  6.5 1.6 copy.15
  8.1 0.0 copy-done.4
  8.1 0.2 fusion
  8.3 0.0 copy-done.14
  8.3 0.0 copy-start.2
  8.3 0.5 convolution_convert_fusion.refs_0_
  8.8 0.0 copy-start.6
  8.8 0.0 copy-done.3
  8.8 0.1 copy.17
  8.9 0.8 copy-done.2
  9.7 1.7 pad_maximum_fusion
  11.5 0.0 all-gather.7.cloned.1.call-update
  11.5 3.1 %collective-permute-start.3 = (bf16[256,512]{1,0:T(8,128)(2,1)S(1)}, bf16[256,512]{1,0:T(8,128)(2,1)S(1)}, u32[]{:S(2)}, u32[]{:S(2)}) collective-permute-start(bf16[256,512]{1,0:T(8,128)(2,1)S(1)} %convolution_convert_fusion.refs_0_), channel_id=1, source_target_pairs={{0,2},{2,4},{4,6},{6,7},{7,5},{5,3},{3,1},{1,0},{8,10},{10,12},{12... | collective-permute-start | bytes 786440 | tf_op jit(solution)/shard_map/ppermute | solution.py:287
  14.6 0.0 copy-done.6
  14.6 0.0 collective-permute-start
  14.6 6.2 %collective-permute-done.3.refs_7_ = bf16[256,512]{1,0:T(8,128)(2,1)S(1)} collective-permute-done((bf16[256,512]{1,0:T(8,128)(2,1)S(1)}, bf16[256,512]{1,0:T(8,128)(2,1)S(1)}, u32[]{:S(2)}, u32[]{:S(2)}) %collective-permute-start.3) | collective-permute-done | bytes 262176 | tf_op jit(solution)/shard_map/ppermute | solution.py:287
  20.8 1.8 collective-permute-start.4
  22.6 0.0 collective-permute-done.refs_1_
  22.6 0.2 collective-permute-start.1
  22.8 5.5 %collective-permute-done.4.refs_6_ = bf16[256,512]{1,0:T(8,128)(2,1)S(1)} collective-permute-done((bf16[256,512]{1,0:T(8,128)(2,1)S(1)}, bf16[256,512]{1,0:T(8,128)(2,1)S(1)}, u32[]{:S(2)}, u32[]{:S(2)}) %collective-permute-start.4) | collective-permute-done | bytes 262176 | tf_op jit(solution)/shard_map/ppermute | solution.py:287
  28.3 1.5 collective-permute-start.5
  29.8 0.0 collective-permute-done.1.refs_2_
  29.8 0.5 collective-permute-start.2
  30.3 4.5 %collective-permute-done.5.refs_5_ = bf16[256,512]{1,0:T(8,128)(2,1)S(1)} collective-permute-done((bf16[256,512]{1,0:T(8,128)(2,1)S(1)}, bf16[256,512]{1,0:T(8,128)(2,1)S(1)}, u32[]{:S(2)}, u32[]{:S(2)}) %collective-permute-start.5) | collective-permute-done | bytes 262176 | tf_op jit(solution)/shard_map/ppermute | solution.py:287
  34.9 1.4 collective-permute-start.6
  36.2 3.1 %constant_dynamic-slice_fusion = bf16[1024,1024]{1,0:T(8,128)(2,1)} fusion(bf16[4096,1024]{1,0:T(8,128)(2,1)} %tokens_ref.3, s32[]{:T(128)S(6)} %select_n.3), kind=kLoop, calls=%fused_computation.11 | loop fusion | bytes 4194308 | tf_op jit(solution)/shard_map/dynamic_slice | solution.py:327
  39.3 0.0 copy-done.7
  39.3 0.0 copy-done.8
  39.4 0.0 copy-done.10
  39.4 0.0 copy-done.11
  39.4 0.0 collective-permute-done.2.refs_3_
  39.4 1.9 collective-permute-done.6.refs_4_
  41.3 0.7 copy-done.13
  42.0 5.6 %all-to-all-start = ((bf16[8,128,1024]{2,1,0:T(8,128)(2,1)}), bf16[8,128,1024]{2,1,0:T(8,128)(2,1)S(1)}, u32[]{:S(2)}, u32[]{:S(2)}) async-start(bf16[8,128,1024]{2,1,0:T(8,128)(2,1)} %bitcast.3), calls=%async_computation | async-start | bytes 4194304 | tf_op jit(solution)/shard_map/all_to_all | solution.py:330
  47.6 0.0 all-gather.5.cloned.1.call-start
  47.6 0.7 copy.12.lists_ref
  48.3 26.7 %cross.1 = bf16[4096,256]{1,0:T(8,128)(2,1)} custom-call(s32[32,8]{1,0:T(8,128)} %copy.12.lists_ref, s32[32]{0:T(128)} %counts_ref.1, s32[1]{0:T(128)} %bitcast.1.tok_ref, bf16[4096,1024]{1,0:T(8,128)(2,1)} %tokens_ref.3, f32[1,1024]{1,0:T(1,128)} %bitcast.30, bf16[1024,256]{1,0:T(8,128)(2,1)} %wq_ref.1, bf16[256,512]{1,0:T(8,128)(2,1)} %copy-done.6, ...), custom_call_target="tpu_custom_call" | custom-call | flops 10737418240 | bytes 10485760 | tf_op jit(solution)/shard_map/cross/pallas_call | solution.py:113
  74.9 17.8 %all-to-all-done.tokens_ref = bf16[8,128,1024]{2,1,0:T(8,128)(2,1)S(1)} async-done(((bf16[8,128,1024]{2,1,0:T(8,128)(2,1)}), bf16[8,128,1024]{2,1,0:T(8,128)(2,1)S(1)}, u32[]{:S(2)}, u32[]{:S(2)}) %all-to-all-start) | async-done | bytes 2097184 | tf_op jit(solution)/shard_map/all_to_all | solution.py:330
  92.8 0.0 all-gather.5.cloned.1.call-update
  92.8 0.0 all-gather.7.cloned.1.call-done
  92.9 1.3 copy-done.1
  94.2 17.9 %view.1 = bf16[4,8,128,256]{3,2,1,0:T(8,128)(2,1)} custom-call(bf16[8,128,1024]{2,1,0:T(8,128)(2,1)} %copy-done.1, f32[1,1024]{1,0:T(1,128)} %bitcast.31, bf16[4,5,1024,256]{3,2,1,0:T(8,128)(2,1)} %bitcast.19, bf16[4,5,1024,256]{3,2,1,0:T(8,128)(2,1)} %bitcast.20), custom_call_target="tpu_custom_call" | custom-call | flops 9663676416 | bytes 12582912 | tf_op jit(solution)/shard_map/view/pallas_call | solution.py:220
  112.0 3.5 %all-to-all-start.1 = ((bf16[32,128,256]{2,1,0:T(8,128)(2,1)}), bf16[32,128,256]{2,1,0:T(8,128)(2,1)S(1)}, u32[]{:S(2)}, u32[]{:S(2)}) async-start(bf16[32,128,256]{2,1,0:T(8,128)(2,1)} %bitcast.25), calls=%async_computation.1 | async-start | bytes 4194304 | tf_op jit(solution)/shard_map/all_to_all | solution.py:338
  115.5 57.1 %all-gather.5.cloned.1.call-done = bf16[16384,256]{1,0:T(8,128)(2,1)} async-done(((bf16[4096,256]{1,0:T(8,128)(2,1)}), bf16[16384,256]{1,0:T(8,128)(2,1)}) %all-gather.5.cloned.1.call-update) | async-done | bytes 8388624 | tf_op jit(solution)/shard_map/all_gather | solution.py:337
  172.6 0.0 all-to-all-done.1
  172.6 1.3 copy-done
  173.9 9.3 %final.1 = bf16[4096,256]{1,0:T(8,128)(2,1)} custom-call(s32[1]{0:T(128)} %bitcast.index_ref, bf16[4096,1024]{1,0:T(8,128)(2,1)} %tokens_ref.3, bf16[4,4096,256]{2,1,0:T(8,128)(2,1)} %bitcast.23, bf16[4096,256]{1,0:T(8,128)(2,1)} %bitcast.22, bf16[4,5,1024,256]{3,2,1,0:T(8,128)(2,1)} %bitcast.21), custom_call_target="tpu_custom_call" | custom-call | flops 2147483648 | bytes 14680064 | tf_op jit(solution)/shard_map/final/pallas_call | solution.py:257
  (17 shorter events, 0.0 us)
Async XLA Ops:
  6.5 1.6 copy-start.4
  6.5 1.8 copy-start.14
  6.5 86.3 %all-gather.7.cloned.1.call-start = ((), (), s32[]{:S(2)}) async-start(), calls=%async_computation.3 | async-start | bytes 13107200 | tf_op jit(solution)/shard_map/all_gather | solution.py:325
  6.5 2.3 %copy-start.3 = (bf16[2,256,1024]{2,1,0:T(8,128)(2,1)S(1)}, bf16[2,256,1024]{2,1,0:T(8,128)(2,1)}, u32[]{:S(2)}) copy-start(bf16[2,256,1024]{2,1,0:T(8,128)(2,1)} %param.15) | copy-start | bytes 3145732
  8.3 1.4 copy-start.2
  8.8 5.8 %copy-start.6 = (bf16[256,512]{1,0:T(8,128)(2,1)}, bf16[256,512]{1,0:T(8,128)(2,1)S(1)}, u32[]{:S(2)}) copy-start(bf16[256,512]{1,0:T(8,128)(2,1)S(1)} %convolution_convert_fusion.refs_0_) | copy-start | bytes 786436
  11.5 9.3 %collective-permute-start.3 = (bf16[256,512]{1,0:T(8,128)(2,1)S(1)}, bf16[256,512]{1,0:T(8,128)(2,1)S(1)}, u32[]{:S(2)}, u32[]{:S(2)}) collective-permute-start(bf16[256,512]{1,0:T(8,128)(2,1)S(1)} %convolution_convert_fusion.refs_0_), channel_id=1, source_target_pairs={{0,2},{2,4},{4,6},{6,7},{7,5},{5,3},{3,1},{1,0},{8,10},{10,12},{12... | collective-permute-start | bytes 786440 | tf_op jit(solution)/shard_map/ppermute | solution.py:287
  14.6 8.0 %collective-permute-start = (bf16[256,512]{1,0:T(8,128)(2,1)S(1)}, bf16[256,512]{1,0:T(8,128)(2,1)S(1)}, u32[]{:S(2)}, u32[]{:S(2)}) collective-permute-start(bf16[256,512]{1,0:T(8,128)(2,1)S(1)} %convolution_convert_fusion.refs_0_), channel_id=1, source_target_pairs={{0,1},{2,0},{4,2},{6,4},{7,6},{5,7},{3,5},{1,3},{8,9},{10,8},{12,1... | collective-permute-start | bytes 786440 | tf_op jit(solution)/shard_map/ppermute | solution.py:289
  20.8 18.5 %copy-start.7 = (bf16[256,512]{1,0:T(8,128)(2,1)}, bf16[256,512]{1,0:T(8,128)(2,1)S(1)}, u32[]{:S(2)}) copy-start(bf16[256,512]{1,0:T(8,128)(2,1)S(1)} %collective-permute-done.3.refs_7_) | copy-start | bytes 786436
  20.8 7.5 %collective-permute-start.4 = (bf16[256,512]{1,0:T(8,128)(2,1)S(1)}, bf16[256,512]{1,0:T(8,128)(2,1)S(1)}, u32[]{:S(2)}, u32[]{:S(2)}) collective-permute-start(bf16[256,512]{1,0:T(8,128)(2,1)S(1)} %collective-permute-done.3.refs_7_), channel_id=1, source_target_pairs={{0,2},{2,4},{4,6},{6,7},{7,5},{5,3},{3,1},{1,0},{8,10},{10,12},{12... | collective-permute-start | bytes 786440 | tf_op jit(solution)/shard_map/ppermute | solution.py:287
  22.6 16.7 %copy-start.8 = (bf16[256,512]{1,0:T(8,128)(2,1)}, bf16[256,512]{1,0:T(8,128)(2,1)S(1)}, u32[]{:S(2)}) copy-start(bf16[256,512]{1,0:T(8,128)(2,1)S(1)} %collective-permute-done.refs_1_) | copy-start | bytes 786436
  22.6 7.2 %collective-permute-start.1 = (bf16[256,512]{1,0:T(8,128)(2,1)S(1)}, bf16[256,512]{1,0:T(8,128)(2,1)S(1)}, u32[]{:S(2)}, u32[]{:S(2)}) collective-permute-start(bf16[256,512]{1,0:T(8,128)(2,1)S(1)} %collective-permute-done.refs_1_), channel_id=1, source_target_pairs={{0,1},{2,0},{4,2},{6,4},{7,6},{5,7},{3,5},{1,3},{8,9},{10,8},{12,1... | collective-permute-start | bytes 786440 | tf_op jit(solution)/shard_map/ppermute | solution.py:289
  28.3 11.0 %copy-start.9 = (bf16[256,512]{1,0:T(8,128)(2,1)}, bf16[256,512]{1,0:T(8,128)(2,1)S(1)}, u32[]{:S(2)}) copy-start(bf16[256,512]{1,0:T(8,128)(2,1)S(1)} %collective-permute-done.4.refs_6_) | copy-start | bytes 786436
  28.3 6.6 %collective-permute-start.5 = (bf16[256,512]{1,0:T(8,128)(2,1)S(1)}, bf16[256,512]{1,0:T(8,128)(2,1)S(1)}, u32[]{:S(2)}, u32[]{:S(2)}) collective-permute-start(bf16[256,512]{1,0:T(8,128)(2,1)S(1)} %collective-permute-done.4.refs_6_), channel_id=1, source_target_pairs={{0,2},{2,4},{4,6},{6,7},{7,5},{5,3},{3,1},{1,0},{8,10},{10,12},{12... | collective-permute-start | bytes 786440 | tf_op jit(solution)/shard_map/ppermute | solution.py:287
  29.8 9.5 %copy-start.10 = (bf16[256,512]{1,0:T(8,128)(2,1)}, bf16[256,512]{1,0:T(8,128)(2,1)S(1)}, u32[]{:S(2)}) copy-start(bf16[256,512]{1,0:T(8,128)(2,1)S(1)} %collective-permute-done.1.refs_2_) | copy-start | bytes 786436
  29.8 9.6 %collective-permute-start.2 = (bf16[256,512]{1,0:T(8,128)(2,1)S(1)}, bf16[256,512]{1,0:T(8,128)(2,1)S(1)}, u32[]{:S(2)}, u32[]{:S(2)}) collective-permute-start(bf16[256,512]{1,0:T(8,128)(2,1)S(1)} %collective-permute-done.1.refs_2_), channel_id=1, source_target_pairs={{0,1},{2,0},{4,2},{6,4},{7,6},{5,7},{3,5},{1,3},{8,9},{10,8},{12,1... | collective-permute-start | bytes 786440 | tf_op jit(solution)/shard_map/ppermute | solution.py:289
  34.9 4.5 %copy-start.11 = (bf16[256,512]{1,0:T(8,128)(2,1)}, bf16[256,512]{1,0:T(8,128)(2,1)S(1)}, u32[]{:S(2)}) copy-start(bf16[256,512]{1,0:T(8,128)(2,1)S(1)} %collective-permute-done.5.refs_5_) | copy-start | bytes 786436
  34.9 6.4 %collective-permute-start.6 = (bf16[256,512]{1,0:T(8,128)(2,1)S(1)}, bf16[256,512]{1,0:T(8,128)(2,1)S(1)}, u32[]{:S(2)}, u32[]{:S(2)}) collective-permute-start(bf16[256,512]{1,0:T(8,128)(2,1)S(1)} %collective-permute-done.5.refs_5_), channel_id=1, source_target_pairs={{0,2},{2,4},{4,6},{6,7},{7,5},{5,3},{3,1},{1,0},{8,10},{10,12},{12... | collective-permute-start | bytes 786440 | tf_op jit(solution)/shard_map/ppermute | solution.py:287
  39.4 1.9 copy-start.12
  41.3 0.7 copy-start.13
  41.3 6.3 %copy-start.5 = (s32[32,8]{0,1:T(8,128)S(1)}, s32[32,8]{0,1:T(8,128)}, u32[]{:S(2)}) copy-start(s32[32,8]{0,1:T(8,128)} %param.16) | copy-start | bytes 3076
  42.0 50.8 %all-to-all-start = ((bf16[8,128,1024]{2,1,0:T(8,128)(2,1)}), bf16[8,128,1024]{2,1,0:T(8,128)(2,1)S(1)}, u32[]{:S(2)}, u32[]{:S(2)}) async-start(bf16[8,128,1024]{2,1,0:T(8,128)(2,1)} %bitcast.3), calls=%async_computation | async-start | bytes 4194304 | tf_op jit(solution)/shard_map/all_to_all | solution.py:330
  47.6 125.0 %all-gather.5.cloned.1.call-start = ((), (), s32[]{:S(2)}) async-start(), calls=%async_computation.2 | async-start | bytes 10485760 | tf_op jit(solution)/shard_map/all_gather | solution.py:337
  92.8 1.4 copy-start.1
  112.0 60.6 %all-to-all-start.1 = ((bf16[32,128,256]{2,1,0:T(8,128)(2,1)}), bf16[32,128,256]{2,1,0:T(8,128)(2,1)S(1)}, u32[]{:S(2)}, u32[]{:S(2)}) async-start(bf16[32,128,256]{2,1,0:T(8,128)(2,1)} %bitcast.25), calls=%async_computation.1 | async-start | bytes 4194304 | tf_op jit(solution)/shard_map/all_to_all | solution.py:338
  172.6 1.3 copy-start
Sparse Core Ops, SparseCore 0:
  11.6 72.8 all-gather.6
  92.9 79.6 all-gather.4

commit v2 on v1

--- a/solution.py
+++ b/solution.py
@@ -13,6 +13,7 @@
 BLOCK = 128
 LOG2_SCALE = math.log2(math.e) / math.sqrt(HD)
 VMEM_BYTES = 60 * 1024 * 1024
+ROOM_VMEM_BYTES = 57 * 1024 * 1024
 CONTRACT_LAST = (((1,), (1,)), ((), ()))
 
 
@@ -233,7 +234,7 @@
             pltpu.VMEM((rows, 3 * cols), jnp.bfloat16),
             pltpu.VMEM((parts, rows, cols), jnp.bfloat16),
         ],
-        compiler_params=pltpu.CompilerParams(vmem_limit_bytes=VMEM_BYTES),
+        compiler_params=pltpu.CompilerParams(vmem_limit_bytes=ROOM_VMEM_BYTES),
         cost_estimate=pl.CostEstimate(
             flops=2 * rows * (parts * cols * (3 * width + 512) + width * width),
             bytes_accessed=2 * (2 * rows * width + 4 * parts * width * cols),
@@ -268,7 +269,7 @@
             ],
             out_specs=own,
         ),
-        compiler_params=pltpu.CompilerParams(vmem_limit_bytes=VMEM_BYTES),
+        compiler_params=pltpu.CompilerParams(vmem_limit_bytes=ROOM_VMEM_BYTES),
         cost_estimate=pl.CostEstimate(
             flops=2 * parts * tok_rows * cols * cols,
             bytes_accessed=2 * tok_rows * cols * (parts + 3),

time: 191 us -> 191 us (level)
  no operation moved by 1% of the time
where the time goes in v2:
time: 191 us; the launch traced here: 190 us
  waiting for transfers between devices  93.1 us (49%)
  Pallas kernels  53.8 us (28%)
  starting transfers between devices  17.6 us (9%)
  between operations  13.5 us (7%)
  local copies, waits for them, and re-layouts  9.6 us (5%)
  other arithmetic  1.94 us (1%)
    all_gather x1, waiting for transfers between devices, shards(): cross_all = lax.all_gather(cross_out, 'head', axis=0, tiled=False)  57.1 us
    pallas_call x1, Pallas kernels, cross_attention(): pl.pallas_call(functools.partial(cross_kernel, halves), out_shape=[jax.Sh...  26.6 us
    ppermute x4, waiting for transfers between devices, ring_chunks(): behind.append(lax.ppermute(behind[-1], 'tok', upward))  18.1 us
    pallas_call x1, Pallas kernels, view_attention(): pl.pallas_call(view_kernel, out_shape=jax.ShapeDtypeStruct((parts, n_tok,...  17.9 us
    all_to_all x1, waiting for transfers between devices, shards(): lax.all_to_all(sent.reshape(n_tok, run, width), 'tok', split_axis=0, conc...  17.9 us
    pallas_call x1, Pallas kernels, final_sum(): pl.pallas_call(final_kernel, out_shape=jax.ShapeDtypeStruct((tok_rows, co...  9.31 us
    ppermute x4, starting transfers between devices, ring_chunks(): behind.append(lax.ppermute(behind[-1], 'tok', upward))  7.76 us
    unnamed x32, local copies, waits for them, and re-layouts  6.42 us
  transfers between devices with their start and end apart: 11, of which 6 were waited for; matrix products, arithmetic and copies ran while one was open for 2% of the time, Pallas kernels for 23%

profile of v2, /device:TPU:0, one launch (start us, length us, event | category | flops | bytes accessed | tf_op | source)
XLA Modules:
  0.0 190.1 jit_solution(1135058106457622404)
XLA Ops:
  6.5 0.0 all-gather.7.cloned.1.call-start
  6.5 1.6 copy.15
  8.1 0.0 copy-done.4
  8.1 0.2 fusion
  8.3 0.0 copy-done.14
  8.3 0.0 copy-start.2
  8.3 0.5 convolution_convert_fusion.refs_0_
  8.8 0.0 copy-start.6
  8.8 0.0 copy-done.3
  8.8 0.1 copy.17
  8.9 0.8 copy-done.2
  9.7 1.7 pad_maximum_fusion
  11.5 0.0 all-gather.7.cloned.1.call-update
  11.5 3.1 %collective-permute-start.3 = (bf16[256,512]{1,0:T(8,128)(2,1)S(1)}, bf16[256,512]{1,0:T(8,128)(2,1)S(1)}, u32[]{:S(2)}, u32[]{:S(2)}) collective-permute-start(bf16[256,512]{1,0:T(8,128)(2,1)S(1)} %convolution_convert_fusion.refs_0_), channel_id=1, source_target_pairs={{0,2},{2,4},{4,6},{6,7},{7,5},{5,3},{3,1},{1,0},{8,10},{10,12},{12... | collective-permute-start | bytes 786440 | tf_op jit(solution)/shard_map/ppermute | solution.py:288
  14.6 0.0 copy-done.6
  14.6 0.0 collective-permute-start
  14.6 6.2 %collective-permute-done.3.refs_7_ = bf16[256,512]{1,0:T(8,128)(2,1)S(1)} collective-permute-done((bf16[256,512]{1,0:T(8,128)(2,1)S(1)}, bf16[256,512]{1,0:T(8,128)(2,1)S(1)}, u32[]{:S(2)}, u32[]{:S(2)}) %collective-permute-start.3) | collective-permute-done | bytes 262176 | tf_op jit(solution)/shard_map/ppermute | solution.py:288
  20.8 1.8 collective-permute-start.4
  22.6 0.0 collective-permute-done.refs_1_
  22.6 0.2 collective-permute-start.1
  22.8 5.5 %collective-permute-done.4.refs_6_ = bf16[256,512]{1,0:T(8,128)(2,1)S(1)} collective-permute-done((bf16[256,512]{1,0:T(8,128)(2,1)S(1)}, bf16[256,512]{1,0:T(8,128)(2,1)S(1)}, u32[]{:S(2)}, u32[]{:S(2)}) %collective-permute-start.4) | collective-permute-done | bytes 262176 | tf_op jit(solution)/shard_map/ppermute | solution.py:288
  28.3 1.5 collective-permute-start.5
  29.8 0.0 collective-permute-done.1.refs_2_
  29.8 0.5 collective-permute-start.2
  30.3 4.5 %collective-permute-done.5.refs_5_ = bf16[256,512]{1,0:T(8,128)(2,1)S(1)} collective-permute-done((bf16[256,512]{1,0:T(8,128)(2,1)S(1)}, bf16[256,512]{1,0:T(8,128)(2,1)S(1)}, u32[]{:S(2)}, u32[]{:S(2)}) %collective-permute-start.5) | collective-permute-done | bytes 262176 | tf_op jit(solution)/shard_map/ppermute | solution.py:288
  34.9 1.4 collective-permute-start.6
  36.2 3.1 %constant_dynamic-slice_fusion = bf16[1024,1024]{1,0:T(8,128)(2,1)} fusion(bf16[4096,1024]{1,0:T(8,128)(2,1)} %tokens_ref.3, s32[]{:T(128)S(6)} %select_n.3), kind=kLoop, calls=%fused_computation.11 | loop fusion | bytes 4194308 | tf_op jit(solution)/shard_map/dynamic_slice | solution.py:328
  39.3 0.0 copy-done.7
  39.3 0.0 copy-done.8
  39.4 0.0 copy-done.10
  39.4 0.0 copy-done.11
  39.4 0.0 collective-permute-done.2.refs_3_
  39.4 1.9 collective-permute-done.6.refs_4_
  41.3 0.7 copy-done.13
  42.0 5.6 %all-to-all-start = ((bf16[8,128,1024]{2,1,0:T(8,128)(2,1)}), bf16[8,128,1024]{2,1,0:T(8,128)(2,1)S(1)}, u32[]{:S(2)}, u32[]{:S(2)}) async-start(bf16[8,128,1024]{2,1,0:T(8,128)(2,1)} %bitcast.3), calls=%async_computation | async-start | bytes 4194304 | tf_op jit(solution)/shard_map/all_to_all | solution.py:331
  47.6 0.0 all-gather.5.cloned.1.call-start
  47.6 0.7 copy.12.lists_ref
  48.3 26.6 %cross.1 = bf16[4096,256]{1,0:T(8,128)(2,1)} custom-call(s32[32,8]{1,0:T(8,128)} %copy.12.lists_ref, s32[32]{0:T(128)} %counts_ref.1, s32[1]{0:T(128)} %bitcast.1.tok_ref, bf16[4096,1024]{1,0:T(8,128)(2,1)} %tokens_ref.3, f32[1,1024]{1,0:T(1,128)} %bitcast.30, bf16[1024,256]{1,0:T(8,128)(2,1)} %wq_ref.1, bf16[256,512]{1,0:T(8,128)(2,1)} %copy-done.6, ...), custom_call_target="tpu_custom_call" | custom-call | flops 10737418240 | bytes 10485760 | tf_op jit(solution)/shard_map/cross/pallas_call | solution.py:114
  74.9 17.9 %all-to-all-done.tokens_ref = bf16[8,128,1024]{2,1,0:T(8,128)(2,1)S(1)} async-done(((bf16[8,128,1024]{2,1,0:T(8,128)(2,1)}), bf16[8,128,1024]{2,1,0:T(8,128)(2,1)S(1)}, u32[]{:S(2)}, u32[]{:S(2)}) %all-to-all-start) | async-done | bytes 2097184 | tf_op jit(solution)/shard_map/all_to_all | solution.py:331
  92.8 0.0 all-gather.5.cloned.1.call-update
  92.8 0.0 all-gather.7.cloned.1.call-done
  92.9 1.3 copy-done.1
  94.2 17.9 %view.1 = bf16[4,8,128,256]{3,2,1,0:T(8,128)(2,1)} custom-call(bf16[8,128,1024]{2,1,0:T(8,128)(2,1)} %copy-done.1, f32[1,1024]{1,0:T(1,128)} %bitcast.31, bf16[4,5,1024,256]{3,2,1,0:T(8,128)(2,1)} %bitcast.19, bf16[4,5,1024,256]{3,2,1,0:T(8,128)(2,1)} %bitcast.20), custom_call_target="tpu_custom_call" | custom-call | flops 9663676416 | bytes 12582912 | tf_op jit(solution)/shard_map/view/pallas_call | solution.py:221
  112.0 3.5 %all-to-all-start.1 = ((bf16[32,128,256]{2,1,0:T(8,128)(2,1)}), bf16[32,128,256]{2,1,0:T(8,128)(2,1)S(1)}, u32[]{:S(2)}, u32[]{:S(2)}) async-start(bf16[32,128,256]{2,1,0:T(8,128)(2,1)} %bitcast.25), calls=%async_computation.1 | async-start | bytes 4194304 | tf_op jit(solution)/shard_map/all_to_all | solution.py:339
  115.5 57.1 %all-gather.5.cloned.1.call-done = bf16[16384,256]{1,0:T(8,128)(2,1)} async-done(((bf16[4096,256]{1,0:T(8,128)(2,1)}), bf16[16384,256]{1,0:T(8,128)(2,1)}) %all-gather.5.cloned.1.call-update) | async-done | bytes 8388624 | tf_op jit(solution)/shard_map/all_gather | solution.py:338
  172.6 0.0 all-to-all-done.1
  172.6 1.3 copy-done
  173.9 9.3 %final.1 = bf16[4096,256]{1,0:T(8,128)(2,1)} custom-call(s32[1]{0:T(128)} %bitcast.index_ref, bf16[4096,1024]{1,0:T(8,128)(2,1)} %tokens_ref.3, bf16[4,4096,256]{2,1,0:T(8,128)(2,1)} %bitcast.23, bf16[4096,256]{1,0:T(8,128)(2,1)} %bitcast.22, bf16[4,5,1024,256]{3,2,1,0:T(8,128)(2,1)} %bitcast.21), custom_call_target="tpu_custom_call" | custom-call | flops 2147483648 | bytes 14680064 | tf_op jit(solution)/shard_map/final/pallas_call | solution.py:258
  (17 shorter events, 0.0 us)
Async XLA Ops:
  6.5 1.6 copy-start.4
  6.5 1.8 copy-start.14
  6.5 86.3 %all-gather.7.cloned.1.call-start = ((), (), s32[]{:S(2)}) async-start(), calls=%async_computation.3 | async-start | bytes 13107200 | tf_op jit(solution)/shard_map/all_gather | solution.py:326
  6.5 2.3 %copy-start.3 = (bf16[2,256,1024]{2,1,0:T(8,128)(2,1)S(1)}, bf16[2,256,1024]{2,1,0:T(8,128)(2,1)}, u32[]{:S(2)}) copy-start(bf16[2,256,1024]{2,1,0:T(8,128)(2,1)} %param.15) | copy-start | bytes 3145732
  8.3 1.4 copy-start.2
  8.8 5.8 %copy-start.6 = (bf16[256,512]{1,0:T(8,128)(2,1)}, bf16[256,512]{1,0:T(8,128)(2,1)S(1)}, u32[]{:S(2)}) copy-start(bf16[256,512]{1,0:T(8,128)(2,1)S(1)} %convolution_convert_fusion.refs_0_) | copy-start | bytes 786436
  11.5 9.3 %collective-permute-start.3 = (bf16[256,512]{1,0:T(8,128)(2,1)S(1)}, bf16[256,512]{1,0:T(8,128)(2,1)S(1)}, u32[]{:S(2)}, u32[]{:S(2)}) collective-permute-start(bf16[256,512]{1,0:T(8,128)(2,1)S(1)} %convolution_convert_fusion.refs_0_), channel_id=1, source_target_pairs={{0,2},{2,4},{4,6},{6,7},{7,5},{5,3},{3,1},{1,0},{8,10},{10,12},{12... | collective-permute-start | bytes 786440 | tf_op jit(solution)/shard_map/ppermute | solution.py:288
  14.6 8.0 %collective-permute-start = (bf16[256,512]{1,0:T(8,128)(2,1)S(1)}, bf16[256,512]{1,0:T(8,128)(2,1)S(1)}, u32[]{:S(2)}, u32[]{:S(2)}) collective-permute-start(bf16[256,512]{1,0:T(8,128)(2,1)S(1)} %convolution_convert_fusion.refs_0_), channel_id=1, source_target_pairs={{0,1},{2,0},{4,2},{6,4},{7,6},{5,7},{3,5},{1,3},{8,9},{10,8},{12,1... | collective-permute-start | bytes 786440 | tf_op jit(solution)/shard_map/ppermute | solution.py:290
  20.8 18.5 %copy-start.7 = (bf16[256,512]{1,0:T(8,128)(2,1)}, bf16[256,512]{1,0:T(8,128)(2,1)S(1)}, u32[]{:S(2)}) copy-start(bf16[256,512]{1,0:T(8,128)(2,1)S(1)} %collective-permute-done.3.refs_7_) | copy-start | bytes 786436
  20.8 7.5 %collective-permute-start.4 = (bf16[256,512]{1,0:T(8,128)(2,1)S(1)}, bf16[256,512]{1,0:T(8,128)(2,1)S(1)}, u32[]{:S(2)}, u32[]{:S(2)}) collective-permute-start(bf16[256,512]{1,0:T(8,128)(2,1)S(1)} %collective-permute-done.3.refs_7_), channel_id=1, source_target_pairs={{0,2},{2,4},{4,6},{6,7},{7,5},{5,3},{3,1},{1,0},{8,10},{10,12},{12... | collective-permute-start | bytes 786440 | tf_op jit(solution)/shard_map/ppermute | solution.py:288
  22.6 16.7 %copy-start.8 = (bf16[256,512]{1,0:T(8,128)(2,1)}, bf16[256,512]{1,0:T(8,128)(2,1)S(1)}, u32[]{:S(2)}) copy-start(bf16[256,512]{1,0:T(8,128)(2,1)S(1)} %collective-permute-done.refs_1_) | copy-start | bytes 786436
  22.6 7.2 %collective-permute-start.1 = (bf16[256,512]{1,0:T(8,128)(2,1)S(1)}, bf16[256,512]{1,0:T(8,128)(2,1)S(1)}, u32[]{:S(2)}, u32[]{:S(2)}) collective-permute-start(bf16[256,512]{1,0:T(8,128)(2,1)S(1)} %collective-permute-done.refs_1_), channel_id=1, source_target_pairs={{0,1},{2,0},{4,2},{6,4},{7,6},{5,7},{3,5},{1,3},{8,9},{10,8},{12,1... | collective-permute-start | bytes 786440 | tf_op jit(solution)/shard_map/ppermute | solution.py:290
  28.3 11.0 %copy-start.9 = (bf16[256,512]{1,0:T(8,128)(2,1)}, bf16[256,512]{1,0:T(8,128)(2,1)S(1)}, u32[]{:S(2)}) copy-start(bf16[256,512]{1,0:T(8,128)(2,1)S(1)} %collective-permute-done.4.refs_6_) | copy-start | bytes 786436
  28.3 6.6 %collective-permute-start.5 = (bf16[256,512]{1,0:T(8,128)(2,1)S(1)}, bf16[256,512]{1,0:T(8,128)(2,1)S(1)}, u32[]{:S(2)}, u32[]{:S(2)}) collective-permute-start(bf16[256,512]{1,0:T(8,128)(2,1)S(1)} %collective-permute-done.4.refs_6_), channel_id=1, source_target_pairs={{0,2},{2,4},{4,6},{6,7},{7,5},{5,3},{3,1},{1,0},{8,10},{10,12},{12... | collective-permute-start | bytes 786440 | tf_op jit(solution)/shard_map/ppermute | solution.py:288
  29.8 9.5 %copy-start.10 = (bf16[256,512]{1,0:T(8,128)(2,1)}, bf16[256,512]{1,0:T(8,128)(2,1)S(1)}, u32[]{:S(2)}) copy-start(bf16[256,512]{1,0:T(8,128)(2,1)S(1)} %collective-permute-done.1.refs_2_) | copy-start | bytes 786436
  29.8 9.6 %collective-permute-start.2 = (bf16[256,512]{1,0:T(8,128)(2,1)S(1)}, bf16[256,512]{1,0:T(8,128)(2,1)S(1)}, u32[]{:S(2)}, u32[]{:S(2)}) collective-permute-start(bf16[256,512]{1,0:T(8,128)(2,1)S(1)} %collective-permute-done.1.refs_2_), channel_id=1, source_target_pairs={{0,1},{2,0},{4,2},{6,4},{7,6},{5,7},{3,5},{1,3},{8,9},{10,8},{12,1... | collective-permute-start | bytes 786440 | tf_op jit(solution)/shard_map/ppermute | solution.py:290
  34.9 4.5 %copy-start.11 = (bf16[256,512]{1,0:T(8,128)(2,1)}, bf16[256,512]{1,0:T(8,128)(2,1)S(1)}, u32[]{:S(2)}) copy-start(bf16[256,512]{1,0:T(8,128)(2,1)S(1)} %collective-permute-done.5.refs_5_) | copy-start | bytes 786436
  34.9 6.4 %collective-permute-start.6 = (bf16[256,512]{1,0:T(8,128)(2,1)S(1)}, bf16[256,512]{1,0:T(8,128)(2,1)S(1)}, u32[]{:S(2)}, u32[]{:S(2)}) collective-permute-start(bf16[256,512]{1,0:T(8,128)(2,1)S(1)} %collective-permute-done.5.refs_5_), channel_id=1, source_target_pairs={{0,2},{2,4},{4,6},{6,7},{7,5},{5,3},{3,1},{1,0},{8,10},{10,12},{12... | collective-permute-start | bytes 786440 | tf_op jit(solution)/shard_map/ppermute | solution.py:288
  39.4 1.9 copy-start.12
  41.3 0.7 copy-start.13
  41.3 6.3 %copy-start.5 = (s32[32,8]{0,1:T(8,128)S(1)}, s32[32,8]{0,1:T(8,128)}, u32[]{:S(2)}) copy-start(s32[32,8]{0,1:T(8,128)} %param.16) | copy-start | bytes 3076
  42.0 50.8 %all-to-all-start = ((bf16[8,128,1024]{2,1,0:T(8,128)(2,1)}), bf16[8,128,1024]{2,1,0:T(8,128)(2,1)S(1)}, u32[]{:S(2)}, u32[]{:S(2)}) async-start(bf16[8,128,1024]{2,1,0:T(8,128)(2,1)} %bitcast.3), calls=%async_computation | async-start | bytes 4194304 | tf_op jit(solution)/shard_map/all_to_all | solution.py:331
  47.6 125.0 %all-gather.5.cloned.1.call-start = ((), (), s32[]{:S(2)}) async-start(), calls=%async_computation.2 | async-start | bytes 10485760 | tf_op jit(solution)/shard_map/all_gather | solution.py:338
  92.8 1.4 copy-start.1
  112.0 60.6 %all-to-all-start.1 = ((bf16[32,128,256]{2,1,0:T(8,128)(2,1)}), bf16[32,128,256]{2,1,0:T(8,128)(2,1)S(1)}, u32[]{:S(2)}, u32[]{:S(2)}) async-start(bf16[32,128,256]{2,1,0:T(8,128)(2,1)} %bitcast.25), calls=%async_computation.1 | async-start | bytes 4194304 | tf_op jit(solution)/shard_map/all_to_all | solution.py:339
  172.6 1.3 copy-start
Sparse Core Ops, SparseCore 0:
  11.6 72.8 all-gather.6
  92.9 79.6 all-gather.4
